TPU v7x, 32 devices: a whole 2x2x4 slice. The times are simulated.
32 devices in a mesh: groups: 2 (over y), pool: 4 (over z), head: 4 (over x, core).
Axes of the slice: x: 2, y: 2, z: 4, core: 2. Of those that a mesh axis runs over, the one named last changes fastest.
Arguments:
- hidden: bfloat16 [1280, 8192], P(('groups', 'pool')), parts along dimension 0, may hold values from -96 to 96
- select: int32 [16, 80], P(('groups', 'pool')), parts along dimension 0, may hold values from 0 to 767, as said below
- page_table: int32 [16, 24], P(('groups', 'pool')), parts along dimension 0, may hold values from -1 to 191, as said below
- kv_store: bfloat16 [384, 32, 2048], P(('groups', 'pool'), None, 'head'), parts along dimension 0, may hold values from -6 to 6
- w_query: bfloat16 [8192, 4096], P('pool', 'head'), may hold values from -0.0625 to 0.0625
- w_kv: bfloat16 [8192, 2048], P('pool', 'head'), may hold values from -0.0625 to 0.0625
Outputs:
- attended: bfloat16 [1280, 4096], P(('groups', 'pool'), 'head'), parts along dimension 0
- new_store: bfloat16 [384, 32, 2048], P(('groups', 'pool'), None, 'head'), parts along dimension 0
There are 2 independent parts, one for each index of `groups`. A program takes and returns all parts, laid end to end along the dimension named above; an argument that names none is the same for every part. Nothing has to cross between parts.
Inputs may be any that keep to these rules, and one draw needn't show every extreme that they name: `page_table`: entry (s, p) is the slot holding page p of session s, held by pool device slot // 48, or -1 where the session is shorter; live entries of a session come first, no slot is named twice, and the live entries of the 2 sessions of one pool device name at most 12 slots of any one holder, a count that is reached. `select`: each row holds 80 distinct increasing positions, all on live pages of its session.
All inputs are finite; a program needn't handle non-finite values.
Results may differ from a plain program's by a relative error of at most 0.0045.
The roundings to bfloat16 on the way count: a program that leaves them out, or rounds other values in their place, can miss the bound.
Values may be sent and summed in bfloat16 or wider, within the bound.
A program may use at most 128 MiB of HBM per device.

v0:
```python
import math

import jax
import jax.numpy as jnp
from jax import lax
from jax.sharding import PartitionSpec as P

HD = 128


ROPE_BASE = 500000.0


def rotate_positions(values, positions):
    half_dim = values.shape[-1] // 2
    exponent = jnp.arange(half_dim, dtype=jnp.float32) * 2.0 / values.shape[-1]
    freqs = jnp.power(jnp.float32(ROPE_BASE), -exponent)
    angles = positions.astype(jnp.float32)[:, None] * freqs[None, :]
    cosine = jnp.cos(angles)[:, None, :]
    sine = jnp.sin(angles)[:, None, :]
    first_half = values[..., :half_dim]
    second_half = values[..., half_dim:]
    return jnp.concatenate(
        [first_half * cosine - second_half * sine, second_half * cosine + first_half * sine],
        axis=-1,
    )


def holder_rank(table_rows, held_slots):
    is_live = table_rows >= 0
    holder_of = jnp.where(is_live, table_rows // held_slots, -1)
    entry_count = table_rows.shape[1]
    earlier_entry = jnp.arange(entry_count)[None, :] < jnp.arange(entry_count)[:, None]
    same_holder = (
        (holder_of[:, :, None] == holder_of[:, None, :]) & earlier_entry[None] & is_live[:, None, :]
    )
    return (is_live, holder_of, jnp.sum(same_holder, axis=2))


def body(hidden, select, page_table, kv_store, w_query, w_kv):
    row_count = hidden.shape[0]
    sessions, pick_count = select.shape
    held_slots, page_len, store_width = kv_store.shape
    local_kv = store_width // (2 * HD)
    local_query = w_query.shape[1] // HD
    group_size = local_query // local_kv
    pool_count = lax.axis_size("pool")
    entry_count = page_table.shape[0] * page_table.shape[1]
    context_len = page_table.shape[1] * page_len
    capacity = max(2, 2 * ((entry_count + 2 * pool_count - 1) // (2 * pool_count)))

    def add_rows(weight_piece):
        return jnp.dot(hidden, weight_piece, preferred_element_type=jnp.float32)

    query_sum = add_rows(lax.all_gather(w_query, "pool", axis=0, tiled=True))
    fresh_sum = add_rows(lax.all_gather(w_kv, "pool", axis=0, tiled=True))
    positions = select.reshape(row_count)
    queries = rotate_positions(query_sum.reshape(row_count, local_query, HD), positions)
    queries = queries.astype(jnp.bfloat16).reshape(sessions, pick_count, local_kv, group_size, HD)
    fresh_pair = fresh_sum.reshape(row_count, local_kv, 2, HD)
    fresh_keys = rotate_positions(fresh_pair[:, :, 0], positions)
    fresh_rows = jnp.stack([fresh_keys, fresh_pair[:, :, 1]], axis=2).astype(jnp.bfloat16)
    fresh_rows = fresh_rows.reshape(sessions, pick_count, store_width)
    own_table = page_table.reshape(1, entry_count)
    live_rows, holder_rows, rank_rows = holder_rank(own_table, held_slots)
    is_live = live_rows[0]
    holder_of = holder_rows[0]
    rank_of = rank_rows[0]
    buffer_size = pool_count * capacity
    target = jnp.where(is_live, holder_of * capacity + rank_of, buffer_size)
    buffer_index = jnp.arange(buffer_size)
    own_slots = own_table[0] % held_slots
    request = jnp.max(
        jnp.where(target[:, None] == buffer_index[None, :], own_slots[:, None], -1), axis=0
    )
    wanted = lax.all_to_all(
        request.reshape(pool_count, capacity), "pool", split_axis=0, concat_axis=0, tiled=True
    )
    safe_slots = jnp.where(wanted >= 0, wanted, 0).reshape(buffer_size)
    outgoing = kv_store[safe_slots].reshape(pool_count, capacity, page_len, store_width)
    arrived = lax.all_to_all(outgoing, "pool", split_axis=0, concat_axis=0, tiled=True).reshape(
        buffer_size, page_len, store_width
    )
    gather_index = jnp.where(is_live, holder_of * capacity + rank_of, 0)
    context = arrived[gather_index].reshape(sessions, context_len, store_width)
    context = context.at[jnp.arange(sessions)[:, None], select].set(fresh_rows)
    split_cache = context.reshape(sessions, context_len, local_kv, 2, HD)
    cache_keys = split_cache[:, :, :, 0]
    cache_values = split_cache[:, :, :, 1]
    scores = jnp.einsum(
        "sikgd,stkd->skgit", queries, cache_keys, preferred_element_type=jnp.float32
    ) / math.sqrt(HD)
    allowed = jnp.arange(context_len)[None, None, :] <= select[:, :, None]
    scores = jnp.where(allowed[:, None, None], scores, -jnp.inf)
    row_peak = jnp.max(scores, axis=-1, keepdims=True)
    exps = jnp.exp(scores - row_peak)
    weights = (exps / jnp.sum(exps, axis=-1, keepdims=True)).astype(jnp.bfloat16)
    attended = jnp.einsum(
        "skgit,stkd->sikgd", weights, cache_values, preferred_element_type=jnp.float32
    )
    attended = attended.astype(jnp.bfloat16).reshape(row_count, local_query * HD)
    returning = jnp.zeros((buffer_size, page_len, store_width), jnp.bfloat16)
    returning = returning.at[target].set(
        context.reshape(entry_count, page_len, store_width), mode="drop"
    )
    returned = lax.all_to_all(
        returning.reshape(pool_count, capacity, page_len, store_width),
        "pool",
        split_axis=0,
        concat_axis=0,
        tiled=True,
    )
    store_target = jnp.where(wanted >= 0, wanted, held_slots).reshape(buffer_size)
    new_store = kv_store.at[store_target].set(
        returned.reshape(buffer_size, page_len, store_width), mode="drop"
    )
    return (attended, new_store)


def solution(mesh):
    return jax.shard_map(
        body,
        mesh=mesh,
        in_specs=(
            P(("groups", "pool"), None),
            P(("groups", "pool"), None),
            P(("groups", "pool"), None),
            P(("groups", "pool"), None, "head"),
            P("pool", "head"),
            P("pool", "head"),
        ),
        out_specs=(P(("groups", "pool"), "head"), P(("groups", "pool"), None, "head")),
        check_vma=False,
    )
```

profile of v0, /device:TPU:2, one launch (start us, length us, event | category | flops | bytes accessed | tf_op | source)
XLA Modules:
  0.0 542.2 jit_solution(9734858420555300071)
XLA Ops:
  7.2 2.9 copy.90
  10.2 0.7 all-gather.5.cloned.1.call-update
  11.7 10.2 %all_to_all.22 = s32[4,1,12]{2,1,0:T(1,128)S(1)} all-to-all(s32[4,1,12]{2,1,0:T(1,128)S(1)} %bitcast.77), channel_id=1, replica_groups=mesh['groups'=2,'pool'=4,'head'=4] {'pool'}, dimensions={0} | all-to-all | bytes 384 | tf_op jit(solution)/shard_map/all_to_all | solution.py:76
  21.9 0.5 broadcast.508
  22.4 0.7 reduce.4
  23.1 3.5 gather_fusion
  26.7 4.5 all-to-all-start.1
  31.6 0.3 multiply_cosine_fusion
  32.0 0.7 copy.64
  32.8 80.7 %all-to-all-done.1 = bf16[4,12,32,512]{3,2,1,0:T(8,128)(2,1)} async-done(((bf16[4,12,32,512]{3,2,1,0:T(8,128)(2,1)}), bf16[4,12,32,512]{3,2,1,0:T(8,128)(2,1)}, u32[]{:S(2)}, u32[]{:S(2)}) %all-to-all-start.1) | async-done | bytes 1572896 | tf_op jit(solution)/shard_map/all_to_all | solution.py:81
  113.4 3.3 gather_fusion.1
  116.8 77.9 %all-gather.3.cloned.1.call-done = bf16[8192,512]{1,0:T(8,128)(2,1)} async-done(((bf16[2048,512]{1,0:T(8,128)(2,1)}), bf16[8192,512]{1,0:T(8,128)(2,1)}) %all-gather.3.cloned.1.call-update) | async-done | bytes 8388624 | tf_op jit(solution)/shard_map/all_gather | solution.py:56
  194.7 4.9 fusion.27
  200.2 1.0 subtract_convert_fusion.1
  201.6 21.1 %scatter_fusion = bf16[2,768,512]{2,1,0:T(8,128)(2,1)} fusion(bf16[2,768,512]{2,1,0:T(8,128)(2,1)} %bitcast.69, s32[160]{0:T(256)S(1)} %reshape.534, bf16[160,512]{1,0:T(8,128)(2,1)S(1)} %reshape.536), kind=kCustom, calls=%fused_computation.2 | custom fusion | bytes 492800 | tf_op jit(solution)/shard_map/scatter | solution.py:86
  222.7 1.3 broadcast_in_dim.40
  224.0 7.4 %scatter_fusion.1 = bf16[48,32,512]{2,1,0:T(8,128)(2,1)} fusion(bf16[48,32,512]{2,1,0:T(8,128)(2,1)} %broadcast_in_dim.40, s32[48]{0:T(128)S(1)} %get-tuple-element.2, bf16[48,32,512]{2,1,0:T(8,128)(2,1)} %bitcast.70), kind=kCustom, calls=%fused_computation.3 | custom fusion | bytes 4718784 | tf_op jit(solution)/shard_map/scatter | solution.py:103
  231.4 4.5 all-to-all-start.2
  235.9 0.8 iota_compare_fusion
  236.7 2.6 copy.67
  239.3 78.6 %all-to-all-done.2 = bf16[4,12,32,512]{3,2,1,0:T(8,128)(2,1)} async-done(((bf16[4,12,32,512]{3,2,1,0:T(8,128)(2,1)}), bf16[4,12,32,512]{3,2,1,0:T(8,128)(2,1)}, u32[]{:S(2)}, u32[]{:S(2)}) %all-to-all-start.2) | async-done | bytes 1572896 | tf_op jit(solution)/shard_map/all_to_all | solution.py:106
  317.9 7.5 %scatter_fusion.2 = bf16[48,32,512]{2,1,0:T(8,128)(2,1)} fusion(bf16[48,32,512]{2,1,0:T(8,128)(2,1)} %copy.90, s32[48]{0:T(128)S(1)} %get-tuple-element.15, bf16[48,32,512]{2,1,0:T(8,128)(2,1)} %bitcast.23), kind=kCustom, calls=%fused_computation.4 | custom fusion | bytes 4718784 | tf_op jit(solution)/shard_map/scatter | solution.py:114
  325.4 189.5 %all-gather.5.cloned.1.call-done = bf16[8192,1024]{1,0:T(8,128)(2,1)} async-done(((bf16[2048,1024]{1,0:T(8,128)(2,1)}), bf16[8192,1024]{1,0:T(8,128)(2,1)}) %all-gather.5.cloned.1.call-update) | async-done | bytes 16777232 | tf_op jit(solution)/shard_map/all_gather | solution.py:55
  514.9 11.1 %fusion.28 = f32[160,1024]{0,1:T(8,128)} fusion(bf16[160,8192]{1,0:T(8,128)(2,1)S(1)} %copy-done, bf16[8192,1024]{1,0:T(8,128)(2,1)} %all-gather.5.cloned.1.call-done), kind=kOutput, calls=%fused_computation.76 | convolution fusion | flops 2684354560 | bytes 20054016 | tf_op jit(solution)/shard_map/reshape | solution.py:58
  526.0 2.0 subtract_convert_fusion
  528.2 0.2 copy.72
  528.4 1.1 concatenate.19
  529.5 0.2 copy.73
  529.8 1.9 fusion.8
  531.7 1.8 fusion.26
  533.5 0.8 fusion.7
  534.4 0.9 reshape.514
  (50 shorter events, 2.6 us)
Async XLA Ops:
  7.2 187.6 %copy-start = (bf16[160,8192]{1,0:T(8,128)(2,1)S(1)}, bf16[160,8192]{1,0:T(8,128)(2,1)}, u32[]{:S(2)}) copy-start(bf16[160,8192]{1,0:T(8,128)(2,1)} %param.6) | copy-start | bytes 7864324
  7.2 187.5 %all-gather.3.cloned.1.call-start = ((), (), s32[]{:S(2)}) async-start(), calls=%async_computation.3 | async-start | bytes 10485760 | tf_op jit(solution)/shard_map/all_gather | solution.py:56
  10.1 0.8 copy-start.4
  10.1 504.8 %all-gather.5.cloned.1.call-start = ((), (), s32[]{:S(2)}) async-start(), calls=%async_computation.4 | async-start | bytes 20971520 | tf_op jit(solution)/shard_map/all_gather | solution.py:55
  26.7 4.7 copy-start.3
  26.7 86.8 %all-to-all-start.1 = ((bf16[4,12,32,512]{3,2,1,0:T(8,128)(2,1)}), bf16[4,12,32,512]{3,2,1,0:T(8,128)(2,1)}, u32[]{:S(2)}, u32[]{:S(2)}) async-start(bf16[4,12,32,512]{3,2,1,0:T(8,128)(2,1)} %bitcast.72), calls=%async_computation.1 | async-start | bytes 3145728 | tf_op jit(solution)/shard_map/all_to_all | solution.py:81
  231.4 86.5 %all-to-all-start.2 = ((bf16[4,12,32,512]{3,2,1,0:T(8,128)(2,1)}), bf16[4,12,32,512]{3,2,1,0:T(8,128)(2,1)}, u32[]{:S(2)}, u32[]{:S(2)}) async-start(bf16[4,12,32,512]{3,2,1,0:T(8,128)(2,1)} %bitcast.71), calls=%async_computation.2 | async-start | bytes 3145728 | tf_op jit(solution)/shard_map/all_to_all | solution.py:106
  529.8 1.9 copy-start.2
  531.7 1.8 copy-start.1
Sparse Core Ops, SparseCore 0:
  10.2 184.4 all-gather.2
  196.3 318.5 all-gather.4
where the time goes:
time: 545 us; the launch traced here: 542 us
  waiting for transfers between devices  427 us (78%)
  local copies, waits for them, and re-layouts  55.5 us (10%)
  matrix products  18.6 us (3%)
  between operations  14.3 us (3%)
  blocking collectives  10.2 us (2%)
  starting transfers between devices  9.07 us (2%)
  other arithmetic  7.12 us (1%)
    all_gather x1, waiting for transfers between devices, body(): query_sum = add_rows(lax.all_gather(w_query, 'pool', axis=0, tiled=True))  190 us
    all_to_all x1, waiting for transfers between devices, body(): lax.all_to_all(outgoing, 'pool', split_axis=0, concat_axis=0, tiled=True)  80.7 us
    all_to_all x1, waiting for transfers between devices, body(): lax.all_to_all(returning.reshape(pool_count, capacity, page_len, store_wi...  78.6 us
    all_gather x1, waiting for transfers between devices, body(): fresh_sum = add_rows(lax.all_gather(w_kv, 'pool', axis=0, tiled=True))  77.9 us
    scatter x2, local copies, waits for them, and re-layouts, body(): context = context.at[jnp.arange(sessions)[:, None], select].set(fresh_rows)  23.7 us
    reshape x1, matrix products, body(): query_sum.reshape(row_count, local_query, HD)  11.1 us
  transfers between devices with their start and end apart: 4, of which 4 were waited for; matrix products, arithmetic and copies ran while one was open for 11% of the time, Pallas kernels for 0%

commit v1 on v0

v1 whole, which is shorter than its diff:
```python
import functools
import math

import jax
import jax.numpy as jnp
from jax import lax
from jax.experimental import pallas as pl
from jax.experimental.pallas import tpu as pltpu
from jax.sharding import PartitionSpec as P

HD = 128
ROPE_BASE = 500000.0
MESH = pl.DeviceIdType.MESH
ANY = pl.BlockSpec(memory_space=pl.ANY)
VMEM = pl.BlockSpec(memory_space=pltpu.VMEM)
SMEM = pl.BlockSpec(memory_space=pltpu.SMEM)
LEVELS = 32700.0
VMEM_BYTES = 56 * 1024 * 1024


def holder_rank(table_rows, held_slots):
    is_live = table_rows >= 0
    holder_of = jnp.where(is_live, table_rows // held_slots, -1)
    entry_count = table_rows.shape[0]
    earlier = jnp.arange(entry_count)[None, :] < jnp.arange(entry_count)[:, None]
    same = (holder_of[:, None] == holder_of[None, :]) & earlier & is_live[None, :]
    return is_live, holder_of, jnp.sum(same, axis=1)


def exchange_kernel(
    pool, heads, share, capacity,
    meta, hidden, wq_hbm, wkv_hbm, store_hbm, own_pick, cosine, sine,
    q_out, fresh_all, pages, meta_all,
    wq, wkv, store, own_x, x_in, acc, part_out, scale_out, part_in, scale_in, page_out, fresh,
    picks,
    load_sem, x_send, x_recv, f_send, f_recv, m_send, m_recv, pick_sem,
    g_send, g_recv, p_send, p_recv, s_send, s_recv, r_send, r_recv, own_sem,
):
    me = lax.axis_index("pool")
    head = lax.axis_index("head")
    depth, q_cols = wq.shape
    kv_cols = wkv.shape[1]
    rows = hidden.shape[0]
    piece = depth // share

    def to(offset):
        return lax.rem(me + offset, pool)

    def frm(offset):
        return lax.rem(me + pool - offset, pool)

    loads = [
        pltpu.make_async_copy(store_hbm, store, load_sem.at[0]),
        pltpu.make_async_copy(
            hidden.at[:, pl.ds(pl.multiple_of(me * depth, depth), depth)], own_x, load_sem.at[1]
        ),
        pltpu.make_async_copy(wq_hbm, wq, load_sem.at[2]),
        pltpu.make_async_copy(wkv_hbm, wkv, load_sem.at[3]),
    ]
    for load in loads:
        load.start()

    barrier = pltpu.get_barrier_semaphore()

    @pl.loop(1, pool)
    def _(offset):
        pl.semaphore_signal(barrier, inc=1, device_id={"pool": to(offset)}, device_id_type=MESH)

    for j in range(1, share):
        pl.semaphore_signal(
            barrier, inc=1, device_id={"head": lax.rem(head + j, heads)}, device_id_type=MESH
        )
    pl.semaphore_wait(barrier, pool - 1 + share - 1)

    def meta_copy(offset):
        return pltpu.make_async_remote_copy(
            src_ref=meta.at[to(offset)], dst_ref=meta_all.at[offset],
            send_sem=m_send.at[offset], recv_sem=m_recv.at[offset],
            device_id={"pool": to(offset)}, device_id_type=MESH,
        )

    def x_copy(offset):
        start = to(offset) * depth
        if share > 1:
            start = start + head * piece
        return pltpu.make_async_remote_copy(
            src_ref=hidden.at[:, pl.ds(pl.multiple_of(start, piece), piece)],
            dst_ref=x_in.at[offset, 0],
            send_sem=x_send.at[offset], recv_sem=x_recv.at[offset],
            device_id={"pool": to(offset)}, device_id_type=MESH,
        )

    def share_copy(offset, j):
        return pltpu.make_async_remote_copy(
            src_ref=x_in.at[offset, 0], dst_ref=x_in.at[offset, j],
            send_sem=f_send.at[offset, j], recv_sem=f_recv.at[offset, j],
            device_id={"head": lax.rem(head + j, heads)}, device_id_type=MESH,
        )

    def page_copy(offset):
        return pltpu.make_async_remote_copy(
            src_ref=page_out.at[offset], dst_ref=pages.at[offset],
            send_sem=g_send.at[offset], recv_sem=g_recv.at[offset],
            device_id={"pool": frm(offset)}, device_id_type=MESH,
        )

    def part_copy(offset):
        return pltpu.make_async_remote_copy(
            src_ref=part_out.at[offset], dst_ref=part_in.at[offset],
            send_sem=p_send.at[offset], recv_sem=p_recv.at[offset],
            device_id={"pool": frm(offset)}, device_id_type=MESH,
        )

    def scale_copy(offset):
        return pltpu.make_async_remote_copy(
            src_ref=scale_out.at[offset], dst_ref=scale_in.at[offset],
            send_sem=s_send.at[offset], recv_sem=s_recv.at[offset],
            device_id={"pool": frm(offset)}, device_id_type=MESH,
        )

    def fresh_copy(offset):
        return pltpu.make_async_remote_copy(
            src_ref=fresh, dst_ref=fresh_all.at[offset],
            send_sem=r_send.at[offset], recv_sem=r_recv.at[offset],
            device_id={"pool": to(offset)}, device_id_type=MESH,
        )

    @pl.loop(1, pool)
    def _(offset):
        meta_copy(offset).start()
        x_copy(offset).start()

    own_meta = pltpu.make_async_copy(meta.at[me], meta_all.at[0], own_sem.at[0])
    own_meta.start()
    loads[0].wait()
    for c in range(capacity):
        page_out[0, c] = store[own_pick[0, c]]
    own_pages = pltpu.make_async_copy(page_out.at[0], pages.at[0], own_sem.at[1])
    own_pages.start()

    def pick_copy(offset):
        return pltpu.make_async_copy(
            meta_all.at[offset, :, pl.ds(0, 128)], picks.at[offset], pick_sem.at[offset]
        )

    @pl.loop(1, pool)
    def _(offset):
        meta_copy(offset).wait_recv()
        pick_copy(offset).start()
        pick_copy(offset).wait()
        for c in range(capacity):
            page_out[offset, c] = store[picks[offset, 0, c]]
        page_copy(offset).start()

    for load in loads[1:]:
        load.wait()
    tile = 256 if q_cols % 256 == 0 and kv_cols % 256 == 0 else 128

    def project(x_of, weight, base):
        @pl.loop(0, weight.shape[1] // tile)
        def _(n):
            cols = pl.ds(pl.multiple_of(n * tile, tile), tile)
            total = None
            for x, start in x_of:
                term = jnp.dot(
                    x[...], weight[pl.ds(start, x.shape[1]), cols],
                    preferred_element_type=jnp.float32,
                )
                total = term if total is None else total + term
            acc[:, pl.ds(pl.multiple_of(base + n * tile, tile), tile)] = total

    if share > 1:
        @pl.loop(1, pool)
        def _(offset):
            x_copy(offset).wait_recv()
            for j in range(1, share):
                share_copy(offset, j).start()

    @pl.loop(1, pool)
    def _(offset):
        pieces = []
        if share > 1:
            for j in range(share):
                if j:
                    share_copy(offset, j).wait_recv()
                start = lax.rem(head + heads - j, heads) * piece
                pieces.append((x_in.at[offset, j], pl.multiple_of(start, piece)))
        else:
            x_copy(offset).wait_recv()
            pieces.append((x_in.at[offset, 0], 0))
        project(pieces, wq, 0)
        project(pieces, wkv, q_cols)
        values = acc[...]
        peak = jnp.max(jnp.abs(values), axis=1, keepdims=True)
        scale = jnp.broadcast_to(jnp.maximum(peak * 1.005, 1e-30), (rows, 128)).astype(jnp.bfloat16)
        scale_out[offset] = scale
        inverse = LEVELS / scale.astype(jnp.float32)
        for n in range((q_cols + kv_cols) // 128):
            coded = jnp.round(acc[:, n * 128:(n + 1) * 128] * inverse)
            part_out[offset, :, n * 128:(n + 1) * 128] = coded.astype(jnp.int32).astype(jnp.int16)
        scale_copy(offset).start()
        part_copy(offset).start()

    project([(own_x, 0)], wq, 0)
    project([(own_x, 0)], wkv, q_cols)

    @pl.loop(1, pool)
    def _(offset):
        scale_copy(offset).wait_recv()
        part_copy(offset).wait_recv()
        factor = scale_in[offset].astype(jnp.float32) * (1.0 / LEVELS)
        for n in range((q_cols + kv_cols) // 128):
            cols = slice(n * 128, (n + 1) * 128)
            acc[:, cols] += part_in[offset, :, cols].astype(jnp.int32).astype(jnp.float32) * factor

    def rotated(cols):
        value = acc[:, cols]
        return (value * cosine[...] + pltpu.roll(value, HD // 2, 1) * sine[...]).astype(jnp.bfloat16)

    for n in range(kv_cols // HD):
        cols = slice(q_cols + n * HD, q_cols + (n + 1) * HD)
        block = rotated(cols) if n % 2 == 0 else acc[:, cols].astype(jnp.bfloat16)
        fresh[:, n * HD:(n + 1) * HD] = block

    @pl.loop(1, pool)
    def _(offset):
        fresh_copy(offset).start()

    own_fresh = pltpu.make_async_copy(fresh, fresh_all.at[0], own_sem.at[2])
    own_fresh.start()
    for n in range(q_cols // HD):
        q_out[:, n * HD:(n + 1) * HD] = rotated(slice(n * HD, (n + 1) * HD))

    own_meta.wait()
    own_pages.wait()
    own_fresh.wait()

    @pl.loop(1, pool)
    def _(offset):
        fresh_copy(offset).wait_recv()
        page_copy(offset).wait_recv()
        meta_copy(offset).wait_send()
        x_copy(offset).wait_send()
        for j in range(1, share):
            share_copy(offset, j).wait_send()
        page_copy(offset).wait_send()
        scale_copy(offset).wait_send()
        part_copy(offset).wait_send()
        fresh_copy(offset).wait_send()


def attend_kernel(
    pool, capacity, first_row_unused,
    gather, base, q, fresh_all, pages, meta_all, store, pos_col, pos_row,
    attended, new_store,
    context,
):
    sessions, context_pages = gather.shape
    page_len, width = store.shape[1:]
    context_len = context_pages * page_len
    rows, q_cols = q.shape
    pick = rows // sessions
    local_kv = width // (2 * HD)
    group = q_cols // HD // local_kv
    for s in range(sessions):
        @pl.loop(0, context_pages)
        def _(p):
            context[pl.ds(pl.multiple_of(p * page_len, page_len), page_len), :] = pages[gather[s, p]]

        token = lax.broadcasted_iota(jnp.int32, (context_len, pick), 0)
        hot = jnp.where(token == pos_row[s], 1.0, 0.0).astype(jnp.bfloat16)
        taken = jnp.dot(hot, jnp.ones((pick, HD), jnp.bfloat16), preferred_element_type=jnp.float32) > 0.5
        mine = fresh_all[0, s * pick:(s + 1) * pick, :]
        for n in range(width // HD):
            cols = slice(n * HD, (n + 1) * HD)
            spread = jnp.dot(hot, mine[:, cols], preferred_element_type=jnp.float32)
            context[:, cols] = jnp.where(
                taken, spread, context[:, cols].astype(jnp.float32)
            ).astype(jnp.bfloat16)
        limit = jnp.concatenate([pos_col[s * pick:(s + 1) * pick, :]] * group, axis=0)
        column = lax.broadcasted_iota(jnp.int32, (group * pick, context_len), 1)
        allowed = column <= limit
        for k in range(local_kv):
            keys = context[:, 2 * k * HD:(2 * k + 1) * HD]
            vals = context[:, (2 * k + 1) * HD:(2 * k + 2) * HD]
            heads = jnp.concatenate(
                [
                    q[s * pick:(s + 1) * pick, (k * group + g) * HD:(k * group + g + 1) * HD]
                    for g in range(group)
                ],
                axis=0,
            )
            scores = lax.dot_general(
                heads, keys, (((1,), (1,)), ((), ())), preferred_element_type=jnp.float32
            ) / math.sqrt(HD)
            scores = jnp.where(allowed, scores, -jnp.inf)
            exps = jnp.exp(scores - jnp.max(scores, axis=1, keepdims=True))
            weights = (exps / jnp.sum(exps, axis=1, keepdims=True)).astype(jnp.bfloat16)
            out = jnp.dot(weights, vals, preferred_element_type=jnp.float32).astype(jnp.bfloat16)
            for g in range(group):
                attended[s * pick:(s + 1) * pick, (k * group + g) * HD:(k * group + g + 1) * HD] = (
                    out[g * pick:(g + 1) * pick]
                )

    held = store.shape[0]
    chunk = next(c for c in (8, 6, 4, 3, 2, 1) if held % c == 0)
    span = chunk * page_len

    @pl.loop(0, held // chunk)
    def _(b):
        slots = pl.ds(b * chunk, chunk)
        place = base[0, 0] + b * span + lax.broadcasted_iota(jnp.int32, (span, rows), 0)
        ones = jnp.ones((rows, HD), jnp.bfloat16)

        def add(offset, carry):
            total, count = carry
            goal = meta_all[offset, 1:2, 0:rows]
            hot = jnp.where(place == goal, 1.0, 0.0).astype(jnp.bfloat16)
            total = total + jnp.dot(hot, fresh_all[offset], preferred_element_type=jnp.float32)
            count = count + jnp.dot(hot, ones, preferred_element_type=jnp.float32)
            return total, count

        total, count = lax.fori_loop(
            0, pool, add,
            (jnp.zeros((span, width), jnp.float32), jnp.zeros((span, HD), jnp.float32)),
        )
        taken = count > 0.5
        for n in range(width // HD):
            cols = slice(n * HD, (n + 1) * HD)
            old = store[slots, :, cols].reshape(span, HD).astype(jnp.float32)
            new = jnp.where(taken, total[:, cols], old).astype(jnp.bfloat16)
            new_store[slots, :, cols] = new.reshape(chunk, page_len, HD)


def body(hidden, select, page_table, kv_store, w_query, w_kv):
    rows = hidden.shape[0]
    sessions, pick_count = select.shape
    held_slots, page_len, width = kv_store.shape
    depth, q_cols = w_query.shape
    kv_cols = w_kv.shape[1]
    pool = lax.axis_size("pool")
    heads = lax.axis_size("head")
    me = lax.axis_index("pool")
    share = heads if depth % (128 * heads) == 0 else 1
    context_pages = page_table.shape[1]
    entry_count = sessions * context_pages
    capacity = max(2, 2 * ((entry_count + 2 * pool - 1) // (2 * pool)))
    lanes = 128 * ((max(rows, capacity) + 127) // 128)

    positions = select.reshape(rows)
    half = HD // 2
    freqs = jnp.power(jnp.float32(ROPE_BASE), -(jnp.arange(half, dtype=jnp.float32) * 2.0 / HD))
    angles = positions.astype(jnp.float32)[:, None] * freqs[None, :]
    cosine = jnp.cos(angles)
    sine = jnp.sin(angles)
    cosine = jnp.concatenate([cosine, cosine], axis=1)
    sine = jnp.concatenate([-sine, sine], axis=1)

    table = page_table.reshape(entry_count)
    is_live, holder_of, rank_of = holder_rank(table, held_slots)
    target = jnp.where(is_live, holder_of * capacity + rank_of, -1)
    own_slots = table % held_slots
    request = jnp.max(
        jnp.where(target[:, None] == jnp.arange(pool * capacity)[None, :], own_slots[:, None], 0),
        axis=0,
    ).reshape(pool, capacity).astype(jnp.int32)
    page_of = select // page_len
    slot_of = jnp.max(
        jnp.where(page_of[:, :, None] == jnp.arange(context_pages)[None, None], page_table[:, None, :], -1),
        axis=2,
    )
    goal = (slot_of * page_len + select % page_len).reshape(1, rows)
    meta = jnp.concatenate(
        [
            jnp.pad(request, ((0, 0), (0, lanes - capacity)))[:, None, :],
            jnp.broadcast_to(jnp.pad(goal, ((0, 0), (0, lanes - rows)))[None], (pool, 1, lanes)),
            jnp.zeros((pool, 6, lanes), jnp.int32),
        ],
        axis=1,
    ).astype(jnp.int32)
    own_pick = lax.dynamic_slice_in_dim(request, me, 1, axis=0)
    relative = jnp.where(is_live, (holder_of - me + pool) % pool, 0)
    gather = jnp.where(is_live, relative * capacity + rank_of, 0).reshape(sessions, context_pages)
    gather = gather.astype(jnp.int32)

    bf16, f32, i32 = jnp.bfloat16, jnp.float32, jnp.int32
    cols = q_cols + kv_cols
    dma = pltpu.SemaphoreType.DMA
    q, fresh_all, pages, meta_all = pl.pallas_call(
        functools.partial(exchange_kernel, pool, heads, share, capacity),
        out_shape=(
            jax.ShapeDtypeStruct((rows, q_cols), bf16),
            jax.ShapeDtypeStruct((pool, rows, kv_cols), bf16),
            jax.ShapeDtypeStruct((pool, capacity, page_len, width), bf16),
            jax.ShapeDtypeStruct((pool, 8, lanes), i32),
        ),
        in_specs=[ANY, ANY, ANY, ANY, ANY, SMEM, VMEM, VMEM],
        out_specs=(VMEM, ANY, ANY, ANY),
        scratch_shapes=[
            pltpu.VMEM((depth, q_cols), bf16),
            pltpu.VMEM((depth, kv_cols), bf16),
            pltpu.VMEM((held_slots, page_len, width), bf16),
            pltpu.VMEM((rows, depth), bf16),
            pltpu.VMEM((pool, share, rows, depth // share), bf16),
            pltpu.VMEM((rows, cols), f32),
            pltpu.VMEM((pool, rows, cols), jnp.int16),
            pltpu.VMEM((pool, rows, 128), bf16),
            pltpu.VMEM((pool, rows, cols), jnp.int16),
            pltpu.VMEM((pool, rows, 128), bf16),
            pltpu.VMEM((pool, capacity, page_len, width), bf16),
            pltpu.VMEM((rows, kv_cols), bf16),
            pltpu.SMEM((pool, 8, 128), i32),
            dma((4,)),
            dma((pool,)), dma((pool,)),
            dma((pool, share)), dma((pool, share)),
            dma((pool,)), dma((pool,)), dma((pool,)),
            dma((pool,)), dma((pool,)),
            dma((pool,)), dma((pool,)),
            dma((pool,)), dma((pool,)),
            dma((pool,)), dma((pool,)),
            dma((3,)),
        ],
        compiler_params=pltpu.CompilerParams(
            collective_id=0, has_side_effects=True, vmem_limit_bytes=VMEM_BYTES
        ),
    )(meta, hidden, w_query, w_kv, kv_store, own_pick, cosine, sine)

    base = (me * held_slots * page_len).astype(i32).reshape(1, 1)
    attended, new_store = pl.pallas_call(
        functools.partial(attend_kernel, pool, capacity, 0),
        out_shape=(
            jax.ShapeDtypeStruct((rows, q_cols), bf16),
            jax.ShapeDtypeStruct(kv_store.shape, bf16),
        ),
        in_specs=[SMEM, SMEM] + [VMEM] * 7,
        out_specs=(VMEM, VMEM),
        scratch_shapes=[pltpu.VMEM((context_pages * page_len, width), bf16)],
        compiler_params=pltpu.CompilerParams(vmem_limit_bytes=VMEM_BYTES),
    )(
        gather, base, q, fresh_all,
        pages.reshape(pool * capacity, page_len, width), meta_all, kv_store,
        select.reshape(rows, 1), select.reshape(sessions, 1, pick_count),
    )
    return attended, new_store


def solution(mesh):
    return jax.shard_map(
        body,
        mesh=mesh,
        in_specs=(
            P(("groups", "pool"), None),
            P(("groups", "pool"), None),
            P(("groups", "pool"), None),
            P(("groups", "pool"), None, "head"),
            P("pool", "head"),
            P("pool", "head"),
        ),
        out_specs=(P(("groups", "pool"), "head"), P(("groups", "pool"), None, "head")),
        check_vma=False,
    )
```

time: 545 us -> 148 us (0.27)
  waiting for transfers between devices: 427 us -> 0 us
  Pallas kernels: 0 us -> 135 us
  local copies, waits for them, and re-layouts: 55.5 us -> 2.83 us
  matrix products: 18.6 us -> 0 us
  between operations: 14.3 us -> 0.68 us
  blocking collectives: 10.2 us -> 0 us
  starting transfers between devices: 9.07 us -> 0 us
    all_gather x2 -> x0, waiting for transfers between devices: 267 us -> none  [the longest x1 190 us: body(): query_sum = add_rows(lax.all_gather(w_query, 'pool', axis=0, tiled=True))]
    all_to_all x2 -> x0, waiting for transfers between devices: 159 us -> none  [the longest x1 80.7 us: body(): lax.all_to_all(outgoing, 'pool', split_axis=0, concat_axis=0, tiled=True)]
    pallas_call x0 -> x2, Pallas kernels: none -> 135 us  [the longest x1 119 us: body(): pl.pallas_call(functools.partial(exchange_kernel, pool, heads, share, cap...]
    scatter x4 -> x0, local copies, waits for them, and re-layouts: 38.6 us -> none  [the longest x2 23.7 us: body(): context = context.at[jnp.arange(sessions)[:, None], select].set(fresh_rows)]
    reshape x1 -> x0, matrix products: 11.1 us -> none  [body(): query_sum.reshape(row_count, local_query, HD)]
    all_to_all x1 -> x0, blocking collectives: 10.2 us -> none  [body(): lax.all_to_all(request.reshape(pool_count, capacity), 'pool', split_axis=...]
    all_to_all x2 -> x0, starting transfers between devices: 8.99 us -> none  [the longest x1 4.52 us: body(): lax.all_to_all(returning.reshape(pool_count, capacity, page_len, store_wi...]
    dot_general x3 -> x0, matrix products: 7.54 us -> none  [the longest x1 4.89 us: add_rows(): return jnp.dot(hidden, weight_piece, preferred_element_type=jnp.float32)]
  transfers between devices with their start and end apart: 4 -> 0, of which waited for: 4 -> 0; matrix products, arithmetic and copies ran while one was open for 11% -> 0% of each run, Pallas kernels for 0% -> 0%
where the time goes in v1:
time: 148 us; the launch traced here: 145 us
  Pallas kernels  135 us (91%)
  other arithmetic  7.01 us (5%)
  local copies, waits for them, and re-layouts  2.83 us (2%)
    pallas_call x1, Pallas kernels, body(): pl.pallas_call(functools.partial(exchange_kernel, pool, heads, share, cap...  119 us
    pallas_call x1, Pallas kernels, body(): pl.pallas_call(functools.partial(attend_kernel, pool, capacity, 0), out_s...  15.1 us

profile of v1, /device:TPU:2, one launch (start us, length us, event | category | flops | bytes accessed | tf_op | source)
XLA Modules:
  0.0 145.0 jit_solution(6136775456012262018)
XLA Ops:
  0.6 0.1 pad.16.clone
  0.7 0.7 and_select_fusion.1
  1.4 0.8 select_reduce_fusion
  2.2 0.8 fusion.8
  3.0 0.1 convert_element_type.15
  3.0 0.1 reshape.124
  3.1 0.7 sign_compare_fusion
  3.8 0.1 ge.28
  3.9 0.1 ne.87
  4.0 0.7 broadcast_remainder_fusion
  4.7 0.1 rem.82
  4.8 0.1 div.40
  4.8 0.2 convert_reduce_fusion
  5.0 0.1 select_reduce_fusion.1
  5.1 0.1 reduce_sum.12
  5.2 1.3 add_select_fusion.gather
  6.5 0.1 reshape.123
  6.6 0.6 constant_dynamic-slice_fusion.own_pick
  7.2 0.7 add_add_fusion.meta
  7.9 1.5 %reshape.128.pos_col = s32[160,1]{1,0:T(8,128)} reshape(s32[2,80]{1,0:T(2,128)} %param.7) | data formatting | bytes 1280 | tf_op jit(solution)/shard_map/reshape | solution.py:350
  9.4 0.4 fusion
  9.7 0.8 pad_maximum_fusion
  10.5 119.4 %shard_map.77 = (bf16[160,1024]{1,0:T(8,128)(2,1)}, bf16[4,160,512]{2,1,0:T(8,128)(2,1)}, bf16[4,12,32,512]{3,2,1,0:T(8,128)(2,1)}, s32[4,8,256]{2,1,0:T(8,128)}) custom-call(s32[4,8,256]{2,1,0:T(8,128)} %add_add_fusion.meta, bf16[160,8192]{1,0:T(8,128)(2,1)} %hidden.1, bf16[2048,1024]{1,0:T(8,128)(2,1)} %wq_hbm.1, bf16[2048,512]{1,0:T(8,128)(2,1)} %wkv_hbm.1, ...), custom_call_target="tpu_custom_call" | custom-call | tf_op jit(solution)/shard_map/pallas_call | solution.py:389
  129.9 15.1 %shard_map.78 = (bf16[160,1024]{1,0:T(8,128)(2,1)}, bf16[48,32,512]{2,1,0:T(8,128)(2,1)}) custom-call(s32[2,24]{1,0:T(2,128)} %add_select_fusion.gather, s32[1,1]{1,0:T(1,128)} %bitcast.base, bf16[160,1024]{1,0:T(8,128)(2,1)} %get-tuple-element.6.q, bf16[4,160,512]{2,1,0:T(8,128)(2,1)} %get-tuple-element.7.fresh_all, bf16[48,32,512]{2,1,0:T(8,128)(2,1)} %bitcast.4, ...), custom_call_target="tpu_custom_call" | custom-call | tf_op jit(solution)/shard_map/pallas_call | solution.py:429
  (8 shorter events, 0.1 us)

commit v2 on v1

--- a/solution.py
+++ b/solution.py
@@ -14,7 +14,7 @@
 ANY = pl.BlockSpec(memory_space=pl.ANY)
 VMEM = pl.BlockSpec(memory_space=pltpu.VMEM)
 SMEM = pl.BlockSpec(memory_space=pltpu.SMEM)
-LEVELS = 32700.0
+LEVELS = 519000.0
 VMEM_BYTES = 56 * 1024 * 1024
 
 
@@ -31,10 +31,11 @@
     pool, heads, share, capacity,
     meta, hidden, wq_hbm, wkv_hbm, store_hbm, own_pick, cosine, sine,
     q_out, fresh_all, pages, meta_all,
-    wq, wkv, store, own_x, x_in, acc, part_out, scale_out, part_in, scale_in, page_out, fresh,
+    wq, wkv, store, own_x, x_in, acc, kv_out, kv_scale, kv_in, kv_scale_in, q_part, q_scale, q_in, q_scale_in,
+    page_out, fresh,
     picks,
     load_sem, x_send, x_recv, f_send, f_recv, m_send, m_recv, pick_sem,
-    g_send, g_recv, p_send, p_recv, s_send, s_recv, r_send, r_recv, own_sem,
+    g_send, g_recv, kv_send, kv_recv, q_send, q_recv, r_send, r_recv, own_sem,
 ):
     me = lax.axis_index("pool")
     head = lax.axis_index("head")
@@ -104,19 +105,18 @@
             device_id={"pool": frm(offset)}, device_id_type=MESH,
         )
 
-    def part_copy(offset):
-        return pltpu.make_async_remote_copy(
-            src_ref=part_out.at[offset], dst_ref=part_in.at[offset],
-            send_sem=p_send.at[offset], recv_sem=p_recv.at[offset],
-            device_id={"pool": frm(offset)}, device_id_type=MESH,
-        )
-
-    def scale_copy(offset):
-        return pltpu.make_async_remote_copy(
-            src_ref=scale_out.at[offset], dst_ref=scale_in.at[offset],
-            send_sem=s_send.at[offset], recv_sem=s_recv.at[offset],
-            device_id={"pool": frm(offset)}, device_id_type=MESH,
-        )
+    def line_copy(bufs, t, going_right):
+        out, scale, inbound, scale_in, send, recv = bufs
+        side = 0 if going_right else 1
+        peer = me + 1 if going_right else me - 1
+        return [
+            pltpu.make_async_remote_copy(
+                src_ref=source.at[t], dst_ref=target.at[side, t],
+                send_sem=send.at[k, t], recv_sem=recv.at[side, k, t],
+                device_id={"pool": peer}, device_id_type=MESH,
+            )
+            for k, (source, target) in enumerate(((scale, scale_in), (out, inbound)))
+        ]
 
     def fresh_copy(offset):
         return pltpu.make_async_remote_copy(
@@ -125,10 +125,24 @@
             device_id={"pool": to(offset)}, device_id_type=MESH,
         )
 
-    @pl.loop(1, pool)
-    def _(offset):
+    def far_first(send, toward):
+        @pl.loop(0, pool - 1)
+        def _(step):
+            distance = pool - 1 - step
+
+            @pl.when(me + distance < pool)
+            def _():
+                send(distance if toward else pool - distance)
+
+            @pl.when(me - distance >= 0)
+            def _():
+                send(pool - distance if toward else distance)
+
+    def send_hidden(offset):
         meta_copy(offset).start()
         x_copy(offset).start()
+
+    far_first(send_hidden, True)
 
     own_meta = pltpu.make_async_copy(meta.at[me], meta_all.at[0], own_sem.at[0])
     own_meta.start()
@@ -170,48 +184,103 @@
             acc[:, pl.ds(pl.multiple_of(base + n * tile, tile), tile)] = total
 
     if share > 1:
-        @pl.loop(1, pool)
-        def _(offset):
+        def pass_on(offset):
             x_copy(offset).wait_recv()
             for j in range(1, share):
                 share_copy(offset, j).start()
 
-    @pl.loop(1, pool)
-    def _(offset):
-        pieces = []
-        if share > 1:
-            for j in range(share):
-                if j:
-                    share_copy(offset, j).wait_recv()
-                start = lax.rem(head + heads - j, heads) * piece
-                pieces.append((x_in.at[offset, j], pl.multiple_of(start, piece)))
-        else:
-            x_copy(offset).wait_recv()
-            pieces.append((x_in.at[offset, 0], 0))
-        project(pieces, wq, 0)
-        project(pieces, wkv, q_cols)
-        values = acc[...]
+        far_first(pass_on, False)
+
+    def encode(bufs, t, base, blocks):
+        values = acc[:, base:base + blocks * 128]
         peak = jnp.max(jnp.abs(values), axis=1, keepdims=True)
         scale = jnp.broadcast_to(jnp.maximum(peak * 1.005, 1e-30), (rows, 128)).astype(jnp.bfloat16)
-        scale_out[offset] = scale
+        bufs[1][t] = scale
         inverse = LEVELS / scale.astype(jnp.float32)
-        for n in range((q_cols + kv_cols) // 128):
-            coded = jnp.round(acc[:, n * 128:(n + 1) * 128] * inverse)
-            part_out[offset, :, n * 128:(n + 1) * 128] = coded.astype(jnp.int32).astype(jnp.int16)
-        scale_copy(offset).start()
-        part_copy(offset).start()
-
-    project([(own_x, 0)], wq, 0)
-    project([(own_x, 0)], wkv, q_cols)
-
-    @pl.loop(1, pool)
-    def _(offset):
-        scale_copy(offset).wait_recv()
-        part_copy(offset).wait_recv()
-        factor = scale_in[offset].astype(jnp.float32) * (1.0 / LEVELS)
-        for n in range((q_cols + kv_cols) // 128):
-            cols = slice(n * 128, (n + 1) * 128)
-            acc[:, cols] += part_in[offset, :, cols].astype(jnp.int32).astype(jnp.float32) * factor
+        for quad in range(0, blocks, 4):
+            packed = jnp.full((rows, 128), -32768, jnp.int32)
+            for n in range(quad, min(quad + 4, blocks)):
+                code = jnp.round(acc[:, base + n * 128:base + (n + 1) * 128] * inverse).astype(jnp.int32)
+                bufs[0][t, :, n * 128:(n + 1) * 128] = (code >> 4).astype(jnp.int16)
+                packed = packed + ((code & 15) << (4 * (n - quad)))
+            lane = (blocks + quad // 4) * 128
+            bufs[0][t, :, lane:lane + 128] = packed.astype(jnp.int16)
+
+    def add_in(bufs, t, side, base, blocks):
+        for copy in line_copy(bufs, t, side == 0):
+            copy.wait_recv()
+        factor = bufs[3][side, t].astype(jnp.float32) * (1.0 / LEVELS)
+        for quad in range(0, blocks, 4):
+            lane = (blocks + quad // 4) * 128
+            packed = bufs[2][side, t, :, lane:lane + 128].astype(jnp.int32) + 32768
+            for n in range(quad, min(quad + 4, blocks)):
+                high = bufs[2][side, t, :, n * 128:(n + 1) * 128].astype(jnp.int32)
+                code = high * 16 + ((packed >> (4 * (n - quad))) & 15)
+                acc[:, base + n * 128:base + (n + 1) * 128] += code.astype(jnp.float32) * factor
+
+    def reduce_line(bufs, weight, base, first):
+        blocks = weight.shape[1] // 128
+
+        def serve(t, going_right):
+            slot = lax.rem(me - t + pool, pool)
+            pieces = []
+            for j in range(share):
+                if first:
+                    if j:
+                        share_copy(slot, j).wait_recv()
+                    elif share == 1:
+                        x_copy(slot).wait_recv()
+                start = pl.multiple_of(lax.rem(head + heads - j, heads) * piece, piece) if share > 1 else 0
+                pieces.append((x_in.at[slot, j], start))
+            project(pieces, weight, base)
+            side = 0 if going_right else 1
+
+            @pl.when(me > 0 if going_right else me < pool - 1)
+            def _():
+                add_in(bufs, t, side, base, blocks)
+
+            encode(bufs, t, base, blocks)
+            for copy in line_copy(bufs, t, going_right):
+                copy.start()
+
+        @pl.loop(0, pool - 1)
+        def _(step):
+            distance = pool - 1 - step
+
+            @pl.when(me + distance < pool)
+            def _():
+                serve(me + distance, True)
+
+            @pl.when(me - distance >= 0)
+            def _():
+                serve(me - distance, False)
+
+        project([(own_x, 0)], weight, base)
+
+        @pl.when(me > 0)
+        def _():
+            add_in(bufs, me, 0, base, blocks)
+
+        @pl.when(me < pool - 1)
+        def _():
+            add_in(bufs, me, 1, base, blocks)
+
+    def finish_line(bufs):
+        @pl.loop(0, pool)
+        def _(t):
+            @pl.when(t > me)
+            def _():
+                for copy in line_copy(bufs, t, True):
+                    copy.wait_send()
+
+            @pl.when(t < me)
+            def _():
+                for copy in line_copy(bufs, t, False):
+                    copy.wait_send()
+
+    kv_bufs = (kv_out, kv_scale, kv_in, kv_scale_in, kv_send, kv_recv)
+    q_bufs = (q_part, q_scale, q_in, q_scale_in, q_send, q_recv)
+    reduce_line(kv_bufs, wkv, q_cols, True)
 
     def rotated(cols):
         value = acc[:, cols]
@@ -228,6 +297,7 @@
 
     own_fresh = pltpu.make_async_copy(fresh, fresh_all.at[0], own_sem.at[2])
     own_fresh.start()
+    reduce_line(q_bufs, wq, 0, False)
     for n in range(q_cols // HD):
         q_out[:, n * HD:(n + 1) * HD] = rotated(slice(n * HD, (n + 1) * HD))
 
@@ -244,9 +314,10 @@
         for j in range(1, share):
             share_copy(offset, j).wait_send()
         page_copy(offset).wait_send()
-        scale_copy(offset).wait_send()
-        part_copy(offset).wait_send()
         fresh_copy(offset).wait_send()
+
+    finish_line(kv_bufs)
+    finish_line(q_bufs)
 
 
 def attend_kernel(
@@ -386,6 +457,16 @@
     bf16, f32, i32 = jnp.bfloat16, jnp.float32, jnp.int32
     cols = q_cols + kv_cols
     dma = pltpu.SemaphoreType.DMA
+
+    def line_scratch(width):
+        coded = width + 128 * ((width // 128 + 3) // 4)
+        return (
+            pltpu.VMEM((pool, rows, coded), jnp.int16),
+            pltpu.VMEM((pool, rows, 128), bf16),
+            pltpu.VMEM((2, pool, rows, coded), jnp.int16),
+            pltpu.VMEM((2, pool, rows, 128), bf16),
+        )
+
     q, fresh_all, pages, meta_all = pl.pallas_call(
         functools.partial(exchange_kernel, pool, heads, share, capacity),
         out_shape=(
@@ -403,10 +484,8 @@
             pltpu.VMEM((rows, depth), bf16),
             pltpu.VMEM((pool, share, rows, depth // share), bf16),
             pltpu.VMEM((rows, cols), f32),
-            pltpu.VMEM((pool, rows, cols), jnp.int16),
-            pltpu.VMEM((pool, rows, 128), bf16),
-            pltpu.VMEM((pool, rows, cols), jnp.int16),
-            pltpu.VMEM((pool, rows, 128), bf16),
+            *line_scratch(kv_cols),
+            *line_scratch(q_cols),
             pltpu.VMEM((pool, capacity, page_len, width), bf16),
             pltpu.VMEM((rows, kv_cols), bf16),
             pltpu.SMEM((pool, 8, 128), i32),
@@ -415,8 +494,8 @@
             dma((pool, share)), dma((pool, share)),
             dma((pool,)), dma((pool,)), dma((pool,)),
             dma((pool,)), dma((pool,)),
-            dma((pool,)), dma((pool,)),
-            dma((pool,)), dma((pool,)),
+            dma((2, pool)), dma((2, 2, pool)),
+            dma((2, pool)), dma((2, 2, pool)),
             dma((pool,)), dma((pool,)),
             dma((3,)),
         ],

time: 148 us -> 138 us (0.932); the launches traced: 145 us -> 138 us
  Pallas kernels: 135 us -> 128 us
    pallas_call x1, Pallas kernels: 119 us -> 112 us  [body(): pl.pallas_call(functools.partial(exchange_kernel, pool, heads, share, cap...]
where the time goes in v2:
time: 138 us
  Pallas kernels  128 us (93%)
  other arithmetic  7.01 us (5%)
  local copies, waits for them, and re-layouts  2.83 us (2%)
    pallas_call x1, Pallas kernels, body(): pl.pallas_call(functools.partial(exchange_kernel, pool, heads, share, cap...  112 us
    pallas_call x1, Pallas kernels, body(): pl.pallas_call(functools.partial(attend_kernel, pool, capacity, 0), out_s...  15.1 us

profile of v2, /device:TPU:2, one launch (start us, length us, event | category | flops | bytes accessed | tf_op | source)
XLA Modules:
  0.0 138.1 jit_solution(6018876714448613397)
XLA Ops:
  0.6 0.1 pad.16.clone
  0.7 0.7 and_select_fusion.1
  1.4 0.8 select_reduce_fusion
  2.2 0.8 fusion.8
  3.0 0.1 convert_element_type.15
  3.0 0.1 reshape.124
  3.1 0.7 sign_compare_fusion
  3.8 0.1 ge.28
  3.9 0.1 ne.87
  4.0 0.7 broadcast_remainder_fusion
  4.7 0.1 rem.82
  4.8 0.1 div.40
  4.8 0.2 convert_reduce_fusion
  5.0 0.1 select_reduce_fusion.1
  5.1 0.1 reduce_sum.12
  5.2 1.3 add_select_fusion.gather
  6.5 0.1 reshape.123
  6.6 0.6 constant_dynamic-slice_fusion.own_pick
  7.2 0.7 add_add_fusion.meta
  7.9 1.5 %reshape.128.pos_col = s32[160,1]{1,0:T(8,128)} reshape(s32[2,80]{1,0:T(2,128)} %param.7) | data formatting | bytes 1280 | tf_op jit(solution)/shard_map/reshape | solution.py:421
  9.4 0.4 fusion
  9.7 0.8 pad_maximum_fusion
  10.5 112.4 %shard_map.77 = (bf16[160,1024]{1,0:T(8,128)(2,1)}, bf16[4,160,512]{2,1,0:T(8,128)(2,1)}, bf16[4,12,32,512]{3,2,1,0:T(8,128)(2,1)}, s32[4,8,256]{2,1,0:T(8,128)}) custom-call(s32[4,8,256]{2,1,0:T(8,128)} %add_add_fusion.meta, bf16[160,8192]{1,0:T(8,128)(2,1)} %hidden.1, bf16[2048,1024]{1,0:T(8,128)(2,1)} %wq_hbm.1, bf16[2048,512]{1,0:T(8,128)(2,1)} %wkv_hbm.1, ...), custom_call_target="tpu_custom_call" | custom-call | tf_op jit(solution)/shard_map/pallas_call | solution.py:470
  123.0 15.1 %shard_map.78 = (bf16[160,1024]{1,0:T(8,128)(2,1)}, bf16[48,32,512]{2,1,0:T(8,128)(2,1)}) custom-call(s32[2,24]{1,0:T(2,128)} %add_select_fusion.gather, s32[1,1]{1,0:T(1,128)} %bitcast.base, bf16[160,1024]{1,0:T(8,128)(2,1)} %get-tuple-element.6.q, bf16[4,160,512]{2,1,0:T(8,128)(2,1)} %get-tuple-element.7.fresh_all, bf16[48,32,512]{2,1,0:T(8,128)(2,1)} %bitcast.4, ...), custom_call_target="tpu_custom_call" | custom-call | tf_op jit(solution)/shard_map/pallas_call | solution.py:508
  (8 shorter events, 0.1 us)

commit v3 on v2

--- a/solution.py
+++ b/solution.py
@@ -31,7 +31,7 @@
     pool, heads, share, capacity,
     meta, hidden, wq_hbm, wkv_hbm, store_hbm, own_pick, cosine, sine,
     q_out, fresh_all, pages, meta_all,
-    wq, wkv, store, own_x, x_in, acc, kv_out, kv_scale, kv_in, kv_scale_in, q_part, q_scale, q_in, q_scale_in,
+    wq, wkv, store, own_x, x_in, acc, own_acc, kv_out, kv_scale, kv_in, kv_scale_in, q_part, q_scale, q_in, q_scale_in,
     page_out, fresh,
     picks,
     load_sem, x_send, x_recv, f_send, f_recv, m_send, m_recv, pick_sem,
@@ -148,7 +148,7 @@
     own_meta.start()
     loads[0].wait()
     for c in range(capacity):
-        page_out[0, c] = store[own_pick[0, c]]
+        page_out[0, c] = store[own_pick[me, c]]
     own_pages = pltpu.make_async_copy(page_out.at[0], pages.at[0], own_sem.at[1])
     own_pages.start()
 
@@ -170,7 +170,7 @@
         load.wait()
     tile = 256 if q_cols % 256 == 0 and kv_cols % 256 == 0 else 128
 
-    def project(x_of, weight, base):
+    def project(target, x_of, weight, base):
         @pl.loop(0, weight.shape[1] // tile)
         def _(n):
             cols = pl.ds(pl.multiple_of(n * tile, tile), tile)
@@ -181,7 +181,10 @@
                     preferred_element_type=jnp.float32,
                 )
                 total = term if total is None else total + term
-            acc[:, pl.ds(pl.multiple_of(base + n * tile, tile), tile)] = total
+            target[:, pl.ds(pl.multiple_of(base + n * tile, tile), tile)] = total
+
+    project(own_acc, [(own_x, 0)], wkv, q_cols)
+    project(own_acc, [(own_x, 0)], wq, 0)
 
     if share > 1:
         def pass_on(offset):
@@ -206,7 +209,7 @@
             lane = (blocks + quad // 4) * 128
             bufs[0][t, :, lane:lane + 128] = packed.astype(jnp.int16)
 
-    def add_in(bufs, t, side, base, blocks):
+    def add_in(target, bufs, t, side, base, blocks):
         for copy in line_copy(bufs, t, side == 0):
             copy.wait_recv()
         factor = bufs[3][side, t].astype(jnp.float32) * (1.0 / LEVELS)
@@ -216,7 +219,7 @@
             for n in range(quad, min(quad + 4, blocks)):
                 high = bufs[2][side, t, :, n * 128:(n + 1) * 128].astype(jnp.int32)
                 code = high * 16 + ((packed >> (4 * (n - quad))) & 15)
-                acc[:, base + n * 128:base + (n + 1) * 128] += code.astype(jnp.float32) * factor
+                target[:, base + n * 128:base + (n + 1) * 128] += code.astype(jnp.float32) * factor
 
     def reduce_line(bufs, weight, base, first):
         blocks = weight.shape[1] // 128
@@ -232,12 +235,12 @@
                         x_copy(slot).wait_recv()
                 start = pl.multiple_of(lax.rem(head + heads - j, heads) * piece, piece) if share > 1 else 0
                 pieces.append((x_in.at[slot, j], start))
-            project(pieces, weight, base)
+            project(acc, pieces, weight, base)
             side = 0 if going_right else 1
 
             @pl.when(me > 0 if going_right else me < pool - 1)
             def _():
-                add_in(bufs, t, side, base, blocks)
+                add_in(acc, bufs, t, side, base, blocks)
 
             encode(bufs, t, base, blocks)
             for copy in line_copy(bufs, t, going_right):
@@ -255,15 +258,13 @@
             def _():
                 serve(me - distance, False)
 
-        project([(own_x, 0)], weight, base)
-
         @pl.when(me > 0)
         def _():
-            add_in(bufs, me, 0, base, blocks)
+            add_in(own_acc, bufs, me, 0, base, blocks)
 
         @pl.when(me < pool - 1)
         def _():
-            add_in(bufs, me, 1, base, blocks)
+            add_in(own_acc, bufs, me, 1, base, blocks)
 
     def finish_line(bufs):
         @pl.loop(0, pool)
@@ -283,12 +284,12 @@
     reduce_line(kv_bufs, wkv, q_cols, True)
 
     def rotated(cols):
-        value = acc[:, cols]
+        value = own_acc[:, cols]
         return (value * cosine[...] + pltpu.roll(value, HD // 2, 1) * sine[...]).astype(jnp.bfloat16)
 
     for n in range(kv_cols // HD):
         cols = slice(q_cols + n * HD, q_cols + (n + 1) * HD)
-        block = rotated(cols) if n % 2 == 0 else acc[:, cols].astype(jnp.bfloat16)
+        block = rotated(cols) if n % 2 == 0 else own_acc[:, cols].astype(jnp.bfloat16)
         fresh[:, n * HD:(n + 1) * HD] = block
 
     @pl.loop(1, pool)
@@ -321,8 +322,8 @@
 
 
 def attend_kernel(
-    pool, capacity, first_row_unused,
-    gather, base, q, fresh_all, pages, meta_all, store, pos_col, pos_row,
+    pool,
+    gather, q, fresh_all, pages, meta_all, store, pos_row,
     attended, new_store,
     context,
 ):
@@ -348,7 +349,13 @@
             context[:, cols] = jnp.where(
                 taken, spread, context[:, cols].astype(jnp.float32)
             ).astype(jnp.bfloat16)
-        limit = jnp.concatenate([pos_col[s * pick:(s + 1) * pick, :]] * group, axis=0)
+        diagonal = lax.broadcasted_iota(jnp.int32, (pick, pick), 0) == lax.broadcasted_iota(
+            jnp.int32, (pick, pick), 1
+        )
+        spot = jnp.sum(
+            jnp.where(diagonal, pos_row[s].astype(jnp.float32), 0.0), axis=1, keepdims=True
+        ).astype(jnp.int32)
+        limit = jnp.concatenate([spot] * group, axis=0)
         column = lax.broadcasted_iota(jnp.int32, (group * pick, context_len), 1)
         allowed = column <= limit
         for k in range(local_kv):
@@ -363,10 +370,10 @@
             )
             scores = lax.dot_general(
                 heads, keys, (((1,), (1,)), ((), ())), preferred_element_type=jnp.float32
-            ) / math.sqrt(HD)
+            ) * (1.0 / math.sqrt(HD))
             scores = jnp.where(allowed, scores, -jnp.inf)
             exps = jnp.exp(scores - jnp.max(scores, axis=1, keepdims=True))
-            weights = (exps / jnp.sum(exps, axis=1, keepdims=True)).astype(jnp.bfloat16)
+            weights = (exps * (1.0 / jnp.sum(exps, axis=1, keepdims=True))).astype(jnp.bfloat16)
             out = jnp.dot(weights, vals, preferred_element_type=jnp.float32).astype(jnp.bfloat16)
             for g in range(group):
                 attended[s * pick:(s + 1) * pick, (k * group + g) * HD:(k * group + g + 1) * HD] = (
@@ -380,7 +387,7 @@
     @pl.loop(0, held // chunk)
     def _(b):
         slots = pl.ds(b * chunk, chunk)
-        place = base[0, 0] + b * span + lax.broadcasted_iota(jnp.int32, (span, rows), 0)
+        place = lax.axis_index("pool") * held * page_len + b * span + lax.broadcasted_iota(jnp.int32, (span, rows), 0)
         ones = jnp.ones((rows, HD), jnp.bfloat16)
 
         def add(offset, carry):
@@ -449,7 +456,6 @@
         ],
         axis=1,
     ).astype(jnp.int32)
-    own_pick = lax.dynamic_slice_in_dim(request, me, 1, axis=0)
     relative = jnp.where(is_live, (holder_of - me + pool) % pool, 0)
     gather = jnp.where(is_live, relative * capacity + rank_of, 0).reshape(sessions, context_pages)
     gather = gather.astype(jnp.int32)
@@ -483,6 +489,7 @@
             pltpu.VMEM((held_slots, page_len, width), bf16),
             pltpu.VMEM((rows, depth), bf16),
             pltpu.VMEM((pool, share, rows, depth // share), bf16),
+            pltpu.VMEM((rows, cols), f32),
             pltpu.VMEM((rows, cols), f32),
             *line_scratch(kv_cols),
             *line_scratch(q_cols),
@@ -502,23 +509,22 @@
         compiler_params=pltpu.CompilerParams(
             collective_id=0, has_side_effects=True, vmem_limit_bytes=VMEM_BYTES
         ),
-    )(meta, hidden, w_query, w_kv, kv_store, own_pick, cosine, sine)
-
-    base = (me * held_slots * page_len).astype(i32).reshape(1, 1)
+    )(meta, hidden, w_query, w_kv, kv_store, request, cosine, sine)
+
     attended, new_store = pl.pallas_call(
-        functools.partial(attend_kernel, pool, capacity, 0),
+        functools.partial(attend_kernel, pool),
         out_shape=(
             jax.ShapeDtypeStruct((rows, q_cols), bf16),
             jax.ShapeDtypeStruct(kv_store.shape, bf16),
         ),
-        in_specs=[SMEM, SMEM] + [VMEM] * 7,
+        in_specs=[SMEM] + [VMEM] * 6,
         out_specs=(VMEM, VMEM),
         scratch_shapes=[pltpu.VMEM((context_pages * page_len, width), bf16)],
         compiler_params=pltpu.CompilerParams(vmem_limit_bytes=VMEM_BYTES),
     )(
-        gather, base, q, fresh_all,
+        gather, q, fresh_all,
         pages.reshape(pool * capacity, page_len, width), meta_all, kv_store,
-        select.reshape(rows, 1), select.reshape(sessions, 1, pick_count),
+        select.reshape(sessions, 1, pick_count),
     )
     return attended, new_store
 

time: 138 us -> 136 us (0.986)
  local copies, waits for them, and re-layouts: 2.83 us -> 0.76 us
    reshape x1 -> x0, local copies, waits for them, and re-layouts: 1.47 us -> none  [body(): positions = select.reshape(rows)]
where the time goes in v3:
time: 136 us
  Pallas kernels  128 us (94%)
  other arithmetic  7 us (5%)
    pallas_call x1, Pallas kernels, body(): pl.pallas_call(functools.partial(exchange_kernel, pool, heads, share, cap...  112 us
    pallas_call x1, Pallas kernels, body(): pl.pallas_call(functools.partial(attend_kernel, pool), out_shape=(jax.Sha...  15.1 us

profile of v3, /device:TPU:2, one launch (start us, length us, event | category | flops | bytes accessed | tf_op | source)
XLA Modules:
  0.0 136.0 jit_solution(12665810290892650717)
XLA Ops:
  0.6 0.1 pad.16.clone
  0.7 0.7 and_select_fusion.1
  1.4 0.8 select_reduce_fusion
  2.2 0.8 fusion.8
  3.0 0.1 convert_element_type.15
  3.0 0.1 reshape.117
  3.1 0.7 sign_compare_fusion
  3.8 0.1 ge.28
  3.9 0.1 ne.87
  4.0 0.7 broadcast_remainder_fusion
  4.7 0.1 rem.82
  4.8 0.1 div.40
  4.8 0.2 convert_reduce_fusion
  5.0 0.1 select_reduce_fusion.1
  5.1 0.1 reduce_sum.12
  5.2 1.3 add_select_fusion.gather
  6.5 0.1 reshape.116.own_pick
  6.6 0.0 copy-start
  6.6 0.7 add_add_fusion.meta
  7.3 0.4 fusion
  7.7 0.8 pad_maximum_fusion
  8.4 0.0 copy-done
  8.4 112.4 %shard_map.77 = (bf16[160,1024]{1,0:T(8,128)(2,1)}, bf16[4,160,512]{2,1,0:T(8,128)(2,1)}, bf16[4,12,32,512]{3,2,1,0:T(8,128)(2,1)}, s32[4,8,256]{2,1,0:T(8,128)}) custom-call(s32[4,8,256]{2,1,0:T(8,128)} %add_add_fusion.meta, bf16[160,8192]{1,0:T(8,128)(2,1)} %hidden.1, bf16[2048,1024]{1,0:T(8,128)(2,1)} %wq_hbm.1, bf16[2048,512]{1,0:T(8,128)(2,1)} %wkv_hbm.1, ...), custom_call_target="tpu_custom_call" | custom-call | tf_op jit(solution)/shard_map/pallas_call | solution.py:476
  120.9 15.1 %shard_map.78 = (bf16[160,1024]{1,0:T(8,128)(2,1)}, bf16[48,32,512]{2,1,0:T(8,128)(2,1)}) custom-call(s32[2,24]{1,0:T(2,128)} %add_select_fusion.gather, bf16[160,1024]{1,0:T(8,128)(2,1)} %get-tuple-element.6.q, bf16[4,160,512]{2,1,0:T(8,128)(2,1)} %get-tuple-element.7.fresh_all, bf16[48,32,512]{2,1,0:T(8,128)(2,1)} %bitcast.3, ...), custom_call_target="tpu_custom_call" | custom-call | tf_op jit(solution)/shard_map/pallas_call | solution.py:514
  (8 shorter events, 0.0 us)
Async XLA Ops:
  6.6 1.9 %copy-start = (s32[4,12]{1,0:T(4,128)}, s32[4,12]{1,0:T(4,128)S(1)}, u32[]{:S(2)}) copy-start(s32[4,12]{1,0:T(4,128)S(1)} %reshape.116.own_pick) | copy-start | bytes 580

commit v4 on v3

--- a/solution.py
+++ b/solution.py
@@ -323,7 +323,7 @@
 
 def attend_kernel(
     pool,
-    gather, q, fresh_all, pages, meta_all, store, pos_row,
+    gather, q, fresh_all, pages, goals, store, pos_row,
     attended, new_store,
     context,
 ):
@@ -342,7 +342,7 @@
         token = lax.broadcasted_iota(jnp.int32, (context_len, pick), 0)
         hot = jnp.where(token == pos_row[s], 1.0, 0.0).astype(jnp.bfloat16)
         taken = jnp.dot(hot, jnp.ones((pick, HD), jnp.bfloat16), preferred_element_type=jnp.float32) > 0.5
-        mine = fresh_all[0, s * pick:(s + 1) * pick, :]
+        mine = fresh_all[s * pick:(s + 1) * pick, :]
         for n in range(width // HD):
             cols = slice(n * HD, (n + 1) * HD)
             spread = jnp.dot(hot, mine[:, cols], preferred_element_type=jnp.float32)
@@ -387,26 +387,18 @@
     @pl.loop(0, held // chunk)
     def _(b):
         slots = pl.ds(b * chunk, chunk)
-        place = lax.axis_index("pool") * held * page_len + b * span + lax.broadcasted_iota(jnp.int32, (span, rows), 0)
-        ones = jnp.ones((rows, HD), jnp.bfloat16)
-
-        def add(offset, carry):
-            total, count = carry
-            goal = meta_all[offset, 1:2, 0:rows]
-            hot = jnp.where(place == goal, 1.0, 0.0).astype(jnp.bfloat16)
-            total = total + jnp.dot(hot, fresh_all[offset], preferred_element_type=jnp.float32)
-            count = count + jnp.dot(hot, ones, preferred_element_type=jnp.float32)
-            return total, count
-
-        total, count = lax.fori_loop(
-            0, pool, add,
-            (jnp.zeros((span, width), jnp.float32), jnp.zeros((span, HD), jnp.float32)),
+        first = lax.axis_index("pool") * held * page_len + b * span
+        place = first + lax.broadcasted_iota(jnp.int32, (span, pool * rows), 0)
+        hot = jnp.where(place == goals[...], 1.0, 0.0).astype(jnp.bfloat16)
+        count = jnp.dot(
+            hot, jnp.ones((pool * rows, HD), jnp.bfloat16), preferred_element_type=jnp.float32
         )
         taken = count > 0.5
         for n in range(width // HD):
             cols = slice(n * HD, (n + 1) * HD)
             old = store[slots, :, cols].reshape(span, HD).astype(jnp.float32)
-            new = jnp.where(taken, total[:, cols], old).astype(jnp.bfloat16)
+            total = jnp.dot(hot, fresh_all[:, cols], preferred_element_type=jnp.float32)
+            new = jnp.where(taken, total, old).astype(jnp.bfloat16)
             new_store[slots, :, cols] = new.reshape(chunk, page_len, HD)
 
 
@@ -511,6 +503,7 @@
         ),
     )(meta, hidden, w_query, w_kv, kv_store, request, cosine, sine)
 
+    goals = meta_all[:, 1, :rows].reshape(1, pool * rows)
     attended, new_store = pl.pallas_call(
         functools.partial(attend_kernel, pool),
         out_shape=(
@@ -522,8 +515,8 @@
         scratch_shapes=[pltpu.VMEM((context_pages * page_len, width), bf16)],
         compiler_params=pltpu.CompilerParams(vmem_limit_bytes=VMEM_BYTES),
     )(
-        gather, q, fresh_all,
-        pages.reshape(pool * capacity, page_len, width), meta_all, kv_store,
+        gather, q, fresh_all.reshape(pool * rows, kv_cols),
+        pages.reshape(pool * capacity, page_len, width), goals, kv_store,
         select.reshape(sessions, 1, pick_count),
     )
     return attended, new_store

time: 136 us -> 133 us (0.978)
  Pallas kernels: 128 us -> 123 us
  local copies, waits for them, and re-layouts: 0.76 us -> 2.21 us
    pallas_call x1, Pallas kernels: 15.1 us -> 10.4 us  [body(): pl.pallas_call(functools.partial(attend_kernel, pool), out_shape=(jax.Sha...]
where the time goes in v4:
time: 133 us
  Pallas kernels  123 us (92%)
  other arithmetic  6.99 us (5%)
  local copies, waits for them, and re-layouts  2.21 us (2%)
    pallas_call x1, Pallas kernels, body(): pl.pallas_call(functools.partial(exchange_kernel, pool, heads, share, cap...  112 us
    pallas_call x1, Pallas kernels, body(): pl.pallas_call(functools.partial(attend_kernel, pool), out_shape=(jax.Sha...  10.4 us

profile of v4, /device:TPU:2, one launch (start us, length us, event | category | flops | bytes accessed | tf_op | source)
XLA Modules:
  0.0 132.7 jit_solution(15346391697739271854)
XLA Ops:
  0.6 0.1 pad.16.clone
  0.7 0.7 and_select_fusion.1
  1.4 0.8 select_reduce_fusion
  2.2 0.8 fusion.8
  3.0 0.1 convert_element_type.15
  3.0 0.1 reshape.120
  3.1 0.7 sign_compare_fusion
  3.8 0.1 ge.28
  3.9 0.1 ne.87
  4.0 0.7 broadcast_remainder_fusion
  4.7 0.1 rem.82
  4.8 0.1 div.40
  4.8 0.2 convert_reduce_fusion
  5.0 0.1 select_reduce_fusion.1
  5.1 0.1 reduce_sum.12
  5.2 1.3 add_select_fusion.gather
  6.5 0.1 reshape.119.own_pick
  6.6 0.0 copy-start
  6.6 0.7 add_add_fusion.meta
  7.3 0.4 fusion
  7.7 0.8 pad_maximum_fusion
  8.4 0.0 copy-done
  8.4 112.4 %shard_map.77 = (bf16[160,1024]{1,0:T(8,128)(2,1)}, bf16[4,160,512]{2,1,0:T(8,128)(2,1)}, bf16[4,12,32,512]{3,2,1,0:T(8,128)(2,1)}, s32[4,8,256]{2,1,0:T(8,128)}) custom-call(s32[4,8,256]{2,1,0:T(8,128)} %add_add_fusion.meta, bf16[160,8192]{1,0:T(8,128)(2,1)} %hidden.1, bf16[2048,1024]{1,0:T(8,128)(2,1)} %wq_hbm.1, bf16[2048,512]{1,0:T(8,128)(2,1)} %wkv_hbm.1, ...), custom_call_target="tpu_custom_call" | custom-call | tf_op jit(solution)/shard_map/pallas_call | solution.py:468
  120.9 0.8 slice_reduce_fusion
  121.7 0.7 reshape_squeeze.3.goals
  122.3 10.4 %shard_map.78 = (bf16[160,1024]{1,0:T(8,128)(2,1)}, bf16[48,32,512]{2,1,0:T(8,128)(2,1)}) custom-call(s32[2,24]{1,0:T(2,128)} %add_select_fusion.gather, bf16[160,1024]{1,0:T(8,128)(2,1)} %get-tuple-element.6.q, bf16[640,512]{1,0:T(8,128)(2,1)} %bitcast.5, bf16[48,32,512]{2,1,0:T(8,128)(2,1)} %bitcast.4, s32[1,640]{1,0:T(1,128)} %reshape_squeeze.3.goals, ...), custom_call_target="tpu_custom_call" | custom-call | tf_op jit(solution)/shard_map/pallas_call | solution.py:507
  (8 shorter events, 0.1 us)
Async XLA Ops:
  6.6 1.8 %copy-start = (s32[4,12]{1,0:T(4,128)}, s32[4,12]{1,0:T(4,128)S(1)}, u32[]{:S(2)}) copy-start(s32[4,12]{1,0:T(4,128)S(1)} %reshape.119.own_pick) | copy-start | bytes 580

commit v5 on v4

--- a/solution.py
+++ b/solution.py
@@ -168,7 +168,7 @@
 
     for load in loads[1:]:
         load.wait()
-    tile = 256 if q_cols % 256 == 0 and kv_cols % 256 == 0 else 128
+    tile = math.gcd(512, math.gcd(q_cols, kv_cols))
 
     def project(target, x_of, weight, base):
         @pl.loop(0, weight.shape[1] // tile)

time: 133 us -> 133 us (level)
  no operation moved by 1% of the time
where the time goes in v5:
time: 133 us
  Pallas kernels  123 us (92%)
  other arithmetic  6.99 us (5%)
  local copies, waits for them, and re-layouts  2.21 us (2%)
    pallas_call x1, Pallas kernels, body(): pl.pallas_call(functools.partial(exchange_kernel, pool, heads, share, cap...  112 us
    pallas_call x1, Pallas kernels, body(): pl.pallas_call(functools.partial(attend_kernel, pool), out_shape=(jax.Sha...  10.4 us

profile of v5, /device:TPU:2, one launch (start us, length us, event | category | flops | bytes accessed | tf_op | source)
XLA Modules:
  0.0 132.7 jit_solution(16743884715692918024)
XLA Ops:
  0.6 0.1 pad.16.clone
  0.7 0.7 and_select_fusion.1
  1.4 0.8 select_reduce_fusion
  2.2 0.8 fusion.8
  3.0 0.1 convert_element_type.15
  3.0 0.1 reshape.120
  3.1 0.7 sign_compare_fusion
  3.8 0.1 ge.28
  3.9 0.1 ne.87
  4.0 0.7 broadcast_remainder_fusion
  4.7 0.1 rem.82
  4.8 0.1 div.40
  4.8 0.2 convert_reduce_fusion
  5.0 0.1 select_reduce_fusion.1
  5.1 0.1 reduce_sum.12
  5.2 1.3 add_select_fusion.gather
  6.5 0.1 reshape.119.own_pick
  6.6 0.0 copy-start
  6.6 0.7 add_add_fusion.meta
  7.3 0.4 fusion
  7.7 0.8 pad_maximum_fusion
  8.4 0.0 copy-done
  8.4 112.4 %shard_map.77 = (bf16[160,1024]{1,0:T(8,128)(2,1)}, bf16[4,160,512]{2,1,0:T(8,128)(2,1)}, bf16[4,12,32,512]{3,2,1,0:T(8,128)(2,1)}, s32[4,8,256]{2,1,0:T(8,128)}) custom-call(s32[4,8,256]{2,1,0:T(8,128)} %add_add_fusion.meta, bf16[160,8192]{1,0:T(8,128)(2,1)} %hidden.1, bf16[2048,1024]{1,0:T(8,128)(2,1)} %wq_hbm.1, bf16[2048,512]{1,0:T(8,128)(2,1)} %wkv_hbm.1, ...), custom_call_target="tpu_custom_call" | custom-call | tf_op jit(solution)/shard_map/pallas_call | solution.py:468
  120.8 0.8 slice_reduce_fusion
  121.6 0.7 reshape_squeeze.3.goals
  122.3 10.4 %shard_map.78 = (bf16[160,1024]{1,0:T(8,128)(2,1)}, bf16[48,32,512]{2,1,0:T(8,128)(2,1)}) custom-call(s32[2,24]{1,0:T(2,128)} %add_select_fusion.gather, bf16[160,1024]{1,0:T(8,128)(2,1)} %get-tuple-element.6.q, bf16[640,512]{1,0:T(8,128)(2,1)} %bitcast.5, bf16[48,32,512]{2,1,0:T(8,128)(2,1)} %bitcast.4, s32[1,640]{1,0:T(1,128)} %reshape_squeeze.3.goals, ...), custom_call_target="tpu_custom_call" | custom-call | tf_op jit(solution)/shard_map/pallas_call | solution.py:507
  (8 shorter events, 0.1 us)
Async XLA Ops:
  6.6 1.8 %copy-start = (s32[4,12]{1,0:T(4,128)}, s32[4,12]{1,0:T(4,128)S(1)}, u32[]{:S(2)}) copy-start(s32[4,12]{1,0:T(4,128)S(1)} %reshape.119.own_pick) | copy-start | bytes 580
